TPU v7x, 256 devices: a whole 4x4x8 slice. The times are simulated.
256 devices in a mesh: corpus: 64 (over z, y, core), pre: 4 (over x).
Axes of the slice: x: 4, y: 4, z: 8, core: 2. Of those that a mesh axis runs over, the one named last changes fastest.
Arguments:
- passages: bfloat16 [4096, 32, 1024], P('corpus'), may hold values from -6 to 6
- query_weight: bfloat16 [1024, 1024], replicated, may hold values from -0.15625 to 0.15625
- kv_weight: bfloat16 [1024, 1024], replicated, may hold values from -0.15625 to 0.15625
- out_weight: bfloat16 [1024, 1024], replicated, may hold values from -1.5 to 1.5
- score_vector: bfloat16 [1024], replicated, may hold values from -0.1875 to 0.1875
- prefix_key_value_state: bfloat16 [64, 2048, 1024], P('corpus', 'pre'), may hold values from -6 to 6
- candidate_owner: int32 [64, 256, 1], P('corpus', 'pre'), may hold values from 0 to 63; in each aligned block of 64 rows (0 to 63, 64 to 127, ..., all dimensions but the last counted through in order) at most 2 rows name the same one
- candidate_row: int32 [64, 256], P('corpus', 'pre'), may hold values from 0 to 63
- candidate_count: int32 [64], P('corpus'), may hold values from 128 to 256, as said below
Outputs:
- scores: float32 [64, 256], P('corpus', 'pre')
Inputs may be any that keep to these rules, and one draw needn't show every extreme that they name: `candidate_owner`: of the 64 slots of one query on one index of pre (slots i * 64 to (i + 1) * 64 - 1), at most 2 name the same owner. `candidate_count`: slots from a query's count on are not live.
All inputs are finite; a program needn't handle non-finite values.
Results may differ from a plain program's by a relative error of at most 0.0075.
Values may be sent and summed in bfloat16 or wider, within the bound.
A program may use at most 128 MiB of HBM per device.

v0:
```python
import jax
import jax.numpy as jnp
from jax import lax
from jax.sharding import PartitionSpec as P

QUERY_HEADS = 8
KEY_VALUE_HEADS = 4
HEAD_SIZE = 128
PREFIX_TOKENS = 2048


epsilon = 1e-06
theta_base = 1000000.0


def rms_rows(value_rows):
    return value_rows * lax.rsqrt(
        jnp.mean(value_rows * value_rows, axis=-1, keepdims=True) + epsilon
    )


def rotate(value_rows, token_positions):
    half_width = value_rows.shape[-1] // 2
    exponent = jnp.arange(half_width, dtype=jnp.float32) * (2.0 / value_rows.shape[-1])
    angles = token_positions.astype(jnp.float32)[:, None] * (theta_base ** (-exponent))[None, :]
    cosine = jnp.cos(angles)[:, None, :]
    sine = jnp.sin(angles)[:, None, :]
    leading = value_rows[..., :half_width]
    trailing = value_rows[..., half_width:]
    return jnp.concatenate(
        [leading * cosine - trailing * sine, trailing * cosine + leading * sine], axis=-1
    )


def turned_keys(unrotated_keys, token_positions):
    reshaped_rows = unrotated_keys.reshape(unrotated_keys.shape[:-1] + (KEY_VALUE_HEADS, HEAD_SIZE))
    return rotate(rms_rows(reshaped_rows), token_positions).astype(jnp.bfloat16)


def passage_states(hidden, kv_weight):
    row_tally = hidden.shape[0]
    prefix_length = hidden.shape[1]
    normed = rms_rows(hidden.astype(jnp.float32)).astype(jnp.bfloat16)
    projected_rows = jnp.dot(
        normed.reshape(row_tally * prefix_length, hidden.shape[2]),
        kv_weight,
        preferred_element_type=jnp.float32,
    )
    projected_rows = projected_rows.reshape(
        row_tally, prefix_length, 2 * KEY_VALUE_HEADS * HEAD_SIZE
    )
    token_positions = PREFIX_TOKENS + jnp.arange(prefix_length, dtype=jnp.int32)
    key_rows = turned_keys(projected_rows[..., : KEY_VALUE_HEADS * HEAD_SIZE], token_positions)
    value_rows = projected_rows[..., KEY_VALUE_HEADS * HEAD_SIZE :].astype(jnp.bfloat16)
    return (key_rows, value_rows)


def last_query(last_hidden, query_weight, prefix_length):
    normed = rms_rows(last_hidden.astype(jnp.float32)).astype(jnp.bfloat16)
    projected_rows = jnp.dot(normed, query_weight, preferred_element_type=jnp.float32)
    reshaped_rows = projected_rows.reshape(last_hidden.shape[0], 1, QUERY_HEADS, HEAD_SIZE)
    position = jnp.full((1,), PREFIX_TOKENS + prefix_length - 1, jnp.int32)
    return rotate(rms_rows(reshaped_rows), position)[:, 0].astype(jnp.bfloat16)


def prefix_terms(query_rows, block_slice):
    prefix_length = block_slice.shape[0]
    key_rows = turned_keys(
        block_slice[:, : KEY_VALUE_HEADS * HEAD_SIZE].astype(jnp.float32),
        jnp.arange(prefix_length, dtype=jnp.int32),
    )
    value_rows = block_slice[:, KEY_VALUE_HEADS * HEAD_SIZE :].reshape(
        prefix_length, KEY_VALUE_HEADS, HEAD_SIZE
    )
    grouped_heads = query_rows.reshape(
        query_rows.shape[0], KEY_VALUE_HEADS, QUERY_HEADS // KEY_VALUE_HEADS, HEAD_SIZE
    )
    logits = jnp.einsum(
        "sghd,pgd->sghp", grouped_heads, key_rows, preferred_element_type=jnp.float32
    ) * HEAD_SIZE ** (-0.5)
    expo = jnp.exp(logits)
    weighted = jnp.einsum(
        "sghp,pgd->sghd", expo.astype(jnp.bfloat16), value_rows, preferred_element_type=jnp.float32
    )
    return (weighted, jnp.sum(expo, axis=-1))


def passage_terms(query_rows, key_rows, value_rows):
    row_tally = query_rows.shape[0]
    grouped_heads = query_rows.reshape(
        row_tally, KEY_VALUE_HEADS, QUERY_HEADS // KEY_VALUE_HEADS, HEAD_SIZE
    )
    logits = jnp.einsum(
        "sghd,stgd->sght", grouped_heads, key_rows, preferred_element_type=jnp.float32
    ) * HEAD_SIZE ** (-0.5)
    expo = jnp.exp(logits)
    reshaped_values = value_rows.reshape(row_tally, value_rows.shape[1], KEY_VALUE_HEADS, HEAD_SIZE)
    weighted = jnp.einsum(
        "sght,stgd->sghd",
        expo.astype(jnp.bfloat16),
        reshaped_values,
        preferred_element_type=jnp.float32,
    )
    return (weighted, jnp.sum(expo, axis=-1))


def finish(weighted, totals, last_hidden, out_weight, score_vector):
    mixed = (
        (weighted / totals[..., None])
        .reshape(weighted.shape[0], QUERY_HEADS * HEAD_SIZE)
        .astype(jnp.bfloat16)
    )
    output = jnp.dot(mixed, out_weight, preferred_element_type=jnp.float32)
    updated = last_hidden.astype(jnp.float32) + output
    return jnp.sum(rms_rows(updated) * score_vector.astype(jnp.float32), axis=-1)


def per_device(
    passages,
    query_weight,
    kv_weight,
    out_weight,
    score_vector,
    prefix_key_value_state,
    candidate_owner,
    candidate_row,
    candidate_count,
):
    owners = candidate_owner[0, :, 0]
    wanted_rows = candidate_row[0]
    slot_count = wanted_rows.shape[0]
    peer_count = lax.axis_size("corpus")
    capacity = max(2, 2 * slot_count // peer_count)
    prefix_length = passages.shape[1]
    width = passages.shape[2]
    matches = (owners[:, None] == jnp.arange(peer_count, dtype=jnp.int32)[None, :]).astype(
        jnp.int32
    )
    position = jnp.sum((jnp.cumsum(matches, axis=0) - matches) * matches, axis=1)
    request = jnp.zeros((peer_count, capacity), jnp.int32).at[owners, position].set(wanted_rows)
    arrived = lax.all_to_all(request, "corpus", split_axis=0, concat_axis=0, tiled=True)
    served = passages[arrived.reshape(-1)]
    returned = lax.all_to_all(
        served.reshape(peer_count, capacity, prefix_length, width),
        "corpus",
        split_axis=0,
        concat_axis=0,
        tiled=True,
    )
    hidden = returned[owners, position]
    key_rows, value_rows = passage_states(hidden, kv_weight)
    last_hidden = hidden[:, -1]
    query_rows = last_query(last_hidden, query_weight, prefix_length)
    weighted, totals = passage_terms(query_rows, key_rows, value_rows)
    part_weighted, part_totals = prefix_terms(
        query_rows, lax.all_gather(prefix_key_value_state, "pre", axis=1, tiled=True)[0]
    )
    result = finish(
        weighted + part_weighted, totals + part_totals, last_hidden, out_weight, score_vector
    )
    slot_index = lax.axis_index("pre") * slot_count + jnp.arange(slot_count, dtype=jnp.int32)
    return jnp.where(slot_index < candidate_count[0], result, jnp.zeros_like(result))[None, :]


def solution(mesh):
    return jax.shard_map(
        per_device,
        mesh=mesh,
        in_specs=(
            P("corpus", None, None),
            P(),
            P(),
            P(),
            P(),
            P("corpus", "pre", None),
            P("corpus", "pre", None),
            P("corpus", "pre"),
            P("corpus"),
        ),
        out_specs=P("corpus", "pre"),
        check_vma=False,
    )
```

profile of v0, /device:TPU:1, one launch (start us, length us, event | category | flops | bytes accessed | tf_op | source)
XLA Modules:
  0.0 296.3 jit_solution(2915884031613394045)
XLA Ops:
  6.5 0.0 copy-start
  6.5 0.9 fusion.40
  7.4 0.1 reduce_window_sum.11
  7.5 0.8 select_reduce_fusion
  8.3 0.7 fusion.43
  9.0 5.8 %scatter_fusion = s32[64,2]{0,1:T(2,128)S(1)} fusion(s32[64,2]{0,1:T(2,128)S(1)} %broadcast_in_dim.4, s32[64]{0:T(128)S(1)} %get-tuple-element.5, s32[64]{0:T(128)} %bitcast.106), kind=kCustom, calls=%fused_computation.2 | custom fusion | bytes 1280 | tf_op jit(solution)/shard_map/scatter | solution.py:140
  14.8 0.1 copy.60
  14.9 22.3 %all_to_all.14 = s32[64,1,2]{2,1,0:T(1,128)S(1)} all-to-all(s32[64,1,2]{2,1,0:T(1,128)S(1)} %copy.60), channel_id=1, replica_groups=mesh['corpus'=64,'pre'=4] {'corpus'}, dimensions={0} | all-to-all | bytes 1024 | tf_op jit(solution)/shard_map/all_to_all | solution.py:141
  37.2 0.5 broadcast.365
  37.7 0.7 reduce.4
  38.5 0.1 reshape.351
  38.6 8.6 %gather_fusion = bf16[128,32,1024]{2,1,0:T(8,128)(2,1)} fusion(bf16[64,32,1024]{2,1,0:T(8,128)(2,1)} %param.9, s32[1024]{0:T(1024)S(1)} %pad_clamp_fusion), kind=kCustom, calls=%fused_computation | custom fusion | bytes 16777728 | tf_op jit(solution)/shard_map/gather | solution.py:142
  47.2 5.9 %all-to-all-start.1 = ((bf16[64,2,32,1024]{3,2,1,0:T(8,128)(2,1)}), bf16[64,2,32,1024]{3,2,1,0:T(8,128)(2,1)}, u32[]{:S(2)}, u32[]{:S(2)}) async-start(bf16[64,2,32,1024]{3,2,1,0:T(8,128)(2,1)} %bitcast.93), calls=%async_computation.1 | async-start | bytes 16777216 | tf_op jit(solution)/shard_map/all_to_all | solution.py:143
  53.1 0.2 all-gather.2.cloned.1.call-start
  53.4 0.0 copy-done.10
  53.4 1.4 copy.68
  54.7 0.0 all-gather.2.cloned.1.call-update
  54.7 0.0 copy-done.11
  55.5 0.1 multiply_cosine_fusion.1
  55.7 5.3 %multiply_cosine_fusion = (f32[2048,64]{1,0:T(8,128)S(1)}, f32[2048,64]{1,0:T(8,128)}) fusion(f32[64]{0:T(128)S(1)} %negate_power_fusion, f32[2048]{0:T(1024)S(1)} %iota_convert_fusion), kind=kLoop, calls=%fused_computation.37 | loop fusion | flops 131072 | bytes 1057024 | tf_op jit(solution)/shard_map/cos | solution.py:26
  61.0 46.6 %all-gather.2.cloned.1.call-done = bf16[1,2048,1024]{1,2,0:T(8,128)(2,1)} async-done(((bf16[1,512,1024]{1,2,0:T(8,128)(2,1)}), bf16[1,2048,1024]{1,2,0:T(8,128)(2,1)}) %all-gather.2.cloned.1.call-update) | async-done | bytes 4194320 | tf_op jit(solution)/shard_map/all_gather | solution.py:156
  107.6 4.8 %fusion.49 = (bf16[2048,512]{0,1:T(8,128)(2,1)}, bf16[2048,512]{0,1:T(8,128)(2,1)}) fusion(bf16[2048,1024]{0,1:T(8,128)(2,1)} %bitcast.94), kind=kLoop, calls=%fused_computation.92 | loop fusion | bytes 8388608 | tf_op jit(solution)/shard_map/slice | solution.py:69
  112.4 4.1 %copy.69 = f32[2048,4,128]{2,0,1:T(8,128)} copy(bf16[2048,4,128]{0,2,1:T(8,128)(2,1)} %bitcast.97) | data formatting | bytes 6291456 | tf_op jit(solution)/shard_map/reshape | solution.py:36
  116.6 2.1 multiply_reduce_fusion
  118.7 3.7 %broadcast_multiply_fusion = f32[2048,4,128]{2,0,1:T(8,128)S(1)} fusion(f32[2048,4,128]{2,0,1:T(8,128)} %copy.69, f32[2048,4]{0,1:T(4,128)S(1)} %add_rsqrt_fusion.1), kind=kLoop, calls=%fused_computation.35 | loop fusion | flops 1048576 | bytes 8421376 | tf_op jit(solution)/shard_map/mul | solution.py:17
  122.4 2.9 subtract_convert_fusion
  125.3 110.8 %all-to-all-done.1 = bf16[64,2,32,1024]{3,2,1,0:T(8,128)(2,1)} async-done(((bf16[64,2,32,1024]{3,2,1,0:T(8,128)(2,1)}), bf16[64,2,32,1024]{3,2,1,0:T(8,128)(2,1)}, u32[]{:S(2)}, u32[]{:S(2)}) %all-to-all-start.1) | async-done | bytes 8388640 | tf_op jit(solution)/shard_map/all_to_all | solution.py:143
  236.0 6.2 %gather_fusion.1 = bf16[64,32,1024]{2,1,0:T(8,128)(2,1)} fusion(bf16[64,2,32,1024]{3,2,1,0:T(8,128)(2,1)} %all-to-all-done.1, s32[64]{0:T(128)S(1)} %bitcast.99), kind=kCustom, calls=%fused_computation.1 | custom fusion | bytes 8389120 | tf_op jit(solution)/shard_map/gather | solution.py:150
  242.2 1.6 slice.51
  243.9 3.2 %fusion = f32[64,32]{1,0:T(8,128)S(1)} fusion(bf16[64,32,1024]{2,1,0:T(8,128)(2,1)} %gather_fusion.1), kind=kLoop, calls=%fused_computation.5 | loop fusion | flops 6289408 | bytes 4202496 | tf_op jit(solution)/shard_map/reduce_sum | solution.py:18
  247.0 0.1 fusion.34
  247.2 0.0 copy-done.6
  247.2 0.5 convolution_bitcast_fusion
  247.7 0.1 multiply_reduce_fusion.4
  247.9 0.1 copy.62
  248.0 0.1 copy.63
  248.1 0.1 broadcast_multiply_fusion.1
  248.2 6.4 %fusion.2 = f32[64,32,1024]{2,1,0:T(8,128)S(1)} fusion(bf16[64,32,1024]{2,1,0:T(8,128)(2,1)} %gather_fusion.1, f32[64,32]{1,0:T(8,128)S(1)} %add_rsqrt_fusion.2, bf16[1024,1024]{1,0:T(8,128)(2,1)S(1)} %copy-done), kind=kOutput, calls=%fused_computation.7 | convolution fusion | flops 4301258752 | bytes 14688256 | tf_op jit(solution)/shard_map/dot_general | solution.py:44
  254.6 4.8 %fusion.48 = (f32[64,32,512]{2,1,0:T(8,128)}, f32[64,4,4,8,128]{4,3,2,1,0:T(8,128)}) fusion(f32[64,32,1024]{2,1,0:T(8,128)S(1)} %fusion.2), kind=kLoop, calls=%fused_computation.91 | loop fusion | bytes 12582912 | tf_op jit(solution)/shard_map/slice | solution.py:53
  259.4 1.0 copy-done.8
  260.4 5.2 %reshape.354 = f32[64,32,4,128]{3,2,1,0:T(4,128)} reshape(f32[64,32,512]{2,1,0:T(8,128)} %get-tuple-element.7) | data formatting | bytes 8388608 | tf_op jit(solution)/shard_map/reshape | solution.py:36
  265.6 4.6 %multiply_reduce_fusion.1 = f32[64,32,4]{2,1,0:T(8,128)S(1)} fusion(f32[64,32,4,128]{3,2,1,0:T(4,128)} %reshape.354), kind=kLoop, calls=%fused_computation.18 | loop fusion | flops 2088960 | bytes 4227072 | tf_op jit(solution)/shard_map/reduce_sum | solution.py:18
  270.3 0.6 copy.64
  270.9 0.1 copy.65
  271.0 0.1 subtract_convert_fusion.2
  271.2 0.1 pad_maximum_fusion
  271.3 0.0 copy-done.3
  271.3 5.2 %bitcast_reduce_fusion = (f32[64,4,2]{0,2,1:T(2,128)S(1)}, f32[4,2048,64,2]{1,2,3,0:T(8,128)}) fusion(bf16[64,4,2,128]{3,2,1,0:T(2,128)(2,1)S(1)} %bitcast.102, bf16[2048,4,64]{2,0,1:T(8,128)(2,1)} %get-tuple-element.10, bf16[2048,4,64]{2,0,1:T(8,128)(2,1)S(1)} %copy-done.3), kind=kOutput, calls=%fused_computation.10 | convolution fusion | flops 274726400 | bytes 6424576 | tf_op jit(solution)/shard_map/sghd,pgd->sghp/dot_general | solution.py:78
  276.6 0.1 copy.73
  276.7 0.0 slice-start
  276.7 3.9 %bitcast_multiply_fusion = f32[64,32,4,128]{3,1,2,0:T(8,128)S(1)} fusion(f32[64,4,4,8,128]{4,3,2,1,0:T(8,128)} %get-tuple-element.8, f32[64,32,4]{1,2,0:T(4,128)S(1)} %copy.65), kind=kLoop, calls=%fused_computation.8 | loop fusion | flops 1048576 | bytes 8421376 | tf_op jit(solution)/shard_map/mul | solution.py:17
  280.6 0.0 slice-start.1
  280.7 1.5 subtract_convert_fusion.1
  282.2 0.0 copy-start.2
  282.2 1.7 fusion.50
  284.0 0.8 copy-done.2
  284.8 0.8 fusion.5
  285.6 0.0 copy-start.1
  285.6 0.7 fusion.31
  286.3 0.1 convert_element_type.85
  286.4 0.2 copy-done.7
  286.5 2.2 multiply_reduce_fusion.3
  288.7 0.2 multiply_reduce_fusion.2
  288.9 0.5 compare_select_fusion.3
  (33 shorter events, 0.3 us)
Async XLA Ops:
  6.5 241.7 %copy-start = (bf16[1024,1024]{1,0:T(8,128)(2,1)S(1)}, bf16[1024,1024]{1,0:T(8,128)(2,1)}, u32[]{:S(2)}) copy-start(bf16[1024,1024]{1,0:T(8,128)(2,1)} %param.11) | copy-start | bytes 6291460
  47.2 6.2 %copy-start.10 = (bf16[1,512,1024]{2,1,0:T(8,128)(2,1)S(1)}, bf16[1,512,1024]{2,1,0:T(8,128)(2,1)}, u32[]{:S(2)}) copy-start(bf16[1,512,1024]{2,1,0:T(8,128)(2,1)} %param.14) | copy-start | bytes 3145732
  47.2 7.6 %copy-start.11 = (bf16[1024]{0:T(1024)(128)(2,1)S(1)}, bf16[1024]{0:T(1024)(128)(2,1)}, u32[]{:S(2)}) copy-start(bf16[1024]{0:T(1024)(128)(2,1)} %param.13) | copy-start | bytes 6148
  47.2 188.8 %all-to-all-start.1 = ((bf16[64,2,32,1024]{3,2,1,0:T(8,128)(2,1)}), bf16[64,2,32,1024]{3,2,1,0:T(8,128)(2,1)}, u32[]{:S(2)}, u32[]{:S(2)}) async-start(bf16[64,2,32,1024]{3,2,1,0:T(8,128)(2,1)} %bitcast.93), calls=%async_computation.1 | async-start | bytes 16777216 | tf_op jit(solution)/shard_map/all_to_all | solution.py:143
  53.1 54.5 %all-gather.2.cloned.1.call-start = ((), (), s32[]{:S(2)}) async-start(), calls=%async_computation.2 | async-start | bytes 5242880 | tf_op jit(solution)/shard_map/all_gather | solution.py:156
  118.7 3.7 %copy-start.5 = (f32[2048,64]{1,0:T(8,128)S(1)}, f32[2048,64]{1,0:T(8,128)}, u32[]{:S(2)}) copy-start(f32[2048,64]{1,0:T(8,128)} %get-tuple-element.18) | copy-start | bytes 1572868
  242.2 5.0 %copy-start.9 = (bf16[1024,1024]{1,0:T(8,128)(2,1)S(1)}, bf16[1024,1024]{1,0:T(8,128)(2,1)}, u32[]{:S(2)}) copy-start(bf16[1024,1024]{1,0:T(8,128)(2,1)} %param.10) | copy-start | bytes 6291460
  243.8 3.3 %copy-start.6 = (bf16[64,1,1024]{2,1,0:T(2,128)(2,1)}, bf16[64,1,1024]{2,1,0:T(2,128)(2,1)S(1)}, u32[]{:S(2)}) copy-start(bf16[64,1,1024]{2,1,0:T(2,128)(2,1)S(1)} %slice.51) | copy-start | bytes 393220
  254.6 5.8 %copy-start.8 = (f32[64,32,1024]{2,1,0:T(8,128)}, f32[64,32,1024]{2,1,0:T(8,128)S(1)}, u32[]{:S(2)}) copy-start(f32[64,32,1024]{2,1,0:T(8,128)S(1)} %fusion.2) | copy-start | bytes 25165828
  265.6 5.7 %copy-start.3 = (bf16[2048,4,64]{2,0,1:T(8,128)(2,1)S(1)}, bf16[2048,4,64]{2,0,1:T(8,128)(2,1)}, u32[]{:S(2)}) copy-start(bf16[2048,4,64]{2,0,1:T(8,128)(2,1)} %get-tuple-element.9) | copy-start | bytes 3145732
  276.7 8.9 %slice-start = ((s8[8388608]{0:T(1024)(128)(4,1)}), s8[4194304]{0:T(1024)(128)(4,1)S(1)}, s32[]{:S(2)}) async-start(s8[8388608]{0:T(1024)(128)(4,1)} %bitcast.100), calls=%async_computation.3 | async-start | bytes 8388608
  280.6 3.3 %copy-start.4 = (bf16[2048,512]{0,1:T(8,128)(2,1)S(1)}, bf16[2048,512]{0,1:T(8,128)(2,1)}, u32[]{:S(2)}) copy-start(bf16[2048,512]{0,1:T(8,128)(2,1)} %get-tuple-element.14) | copy-start | bytes 6291460
  280.6 5.0 %slice-start.1 = ((s8[8388608]{0:T(1024)(128)(4,1)}), s8[4194304]{0:T(1024)(128)(4,1)S(1)}, s32[]{:S(2)}) async-start(s8[8388608]{0:T(1024)(128)(4,1)} %bitcast.100), calls=%async_computation.4 | async-start | bytes 8388608
  282.2 2.6 copy-start.2
  285.6 1.0 copy-start.7
  285.6 3.9 %copy-start.1 = (bf16[1024,1024]{1,0:T(8,128)(2,1)S(1)}, bf16[1024,1024]{1,0:T(8,128)(2,1)}, u32[]{:S(2)}) copy-start(bf16[1024,1024]{1,0:T(8,128)(2,1)} %param.11) | copy-start | bytes 6291460
Sparse Core Ops, SparseCore 0:
  55.8 51.7 all-gather.1
where the time goes:
time: 299 us; the launch traced here: 296 us
  waiting for transfers between devices  157 us (53%)
  local copies, waits for them, and re-layouts  46.3 us (15%)
  other arithmetic  32.1 us (11%)
  blocking collectives  22.3 us (7%)
  matrix products  17.5 us (6%)
  between operations  14.5 us (5%)
  starting transfers between devices  6.16 us (2%)
    all_to_all x1, waiting for transfers between devices, per_device(): lax.all_to_all(served.reshape(peer_count, capacity, prefix_length, width)...  111 us
    all_gather x1, waiting for transfers between devices, per_device(): lax.all_gather(prefix_key_value_state, 'pre', axis=1, tiled=True)[0]  46.6 us
    all_to_all x1, blocking collectives, per_device(): lax.all_to_all(request, 'corpus', split_axis=0, concat_axis=0, tiled=True)  22.3 us
    reduce_sum x5, other arithmetic, rms_rows(): jnp.mean(value_rows * value_rows, axis=-1, keepdims=True) + epsilon  10.1 us
    reshape x2, local copies, waits for them, and re-layouts, turned_keys(): unrotated_keys.reshape(unrotated_keys.shape[:-1] + (KEY_VALUE_HEADS, HEAD...  9.36 us
    gather x1, local copies, waits for them, and re-layouts, per_device(): served = passages[arrived.reshape(-1)]  8.56 us
    mul x3, other arithmetic, rms_rows(): value_rows * lax.rsqrt(jnp.mean(value_rows * value_rows, axis=-1, keepdim...  7.73 us
    dot_general x1, matrix products, passage_states(): jnp.dot(normed.reshape(row_tally * prefix_length, hidden.shape[2]), kv_we...  6.38 us
  transfers between devices with their start and end apart: 2, of which 2 were waited for; matrix products, arithmetic and copies ran while one was open for 8% of the time, Pallas kernels for 0%

commit v1 on v0

v1 whole, which is shorter than its diff:
```python
import jax
import jax.numpy as jnp
import numpy as np
from jax import lax
from jax.experimental import pallas as pl
from jax.experimental.pallas import tpu as pltpu
from jax.sharding import PartitionSpec as P

MESH = pl.DeviceIdType.MESH
BF = jnp.bfloat16
F32 = jnp.float32

OWNERS = 64
PRE = 4
SLOTS = 64
PASS = 64
TOKENS = 32
WIDTH = 1024
HEADS = 8
GROUPS = 4
HEAD = 128
PREFIX = 2048
SHARE = PREFIX // PRE
CHUNK = 512
CHUNK_PASS = CHUNK // TOKENS
SCALE = HEAD**-0.5
EPS = 1e-06
PART = HEAD + 16


def angle_table():
    half = HEAD // 2
    exponent = np.arange(half, dtype=np.float32) * np.float32(2.0 / HEAD)
    freq = np.float32(1000000.0) ** (-exponent)
    angles = np.arange(PREFIX + TOKENS, dtype=np.float32)[:, None] * freq[None, :]
    angles = angles.astype(np.float64)
    return np.concatenate([np.cos(angles), np.sin(angles)], axis=1).astype(np.float32)


def iota(shape, dim):
    return lax.broadcasted_iota(jnp.int32, shape, dim)


def cos_sin(table):
    swapped = pltpu.roll(table, HEAD // 2, 1)
    low = iota(table.shape, 1) < HEAD // 2
    return jnp.where(low, table, swapped), jnp.where(low, -swapped, table)


def unit(rows):
    return rows * lax.rsqrt(jnp.mean(rows * rows, axis=-1, keepdims=True) + EPS)


def turn(rows, cosine, sine):
    return rows * cosine + pltpu.roll(rows, HEAD // 2, 1) * sine


def dot(a, b):
    return jnp.dot(a, b, preferred_element_type=F32)


def dot_t(a, b):
    return lax.dot_general(a, b, (((1,), (1,)), ((), ())), preferred_element_type=F32)


def split_two(total):
    high = total.astype(BF).astype(F32)
    return high, total - high


def kernel(
    passages, query_weight, kv_weight, out_weight, score_vector, prefix, table,
    owner_col, owner_row, row_row, count, out,
    pas, wq, wkv, wo, pre_v, tab, tail,
    last32, own_rows, own_sums, own_tots, own_query, own_tot,
    pre_keys, req_out, req_in, pick, place,
    last_out, last_in, sums_out, sums_in, query_all, part_out, part_in, slot_last,
    load_sem, send_sem, recv_sem,
):
    me = lax.axis_index("corpus")
    px = lax.axis_index("pre")

    loads = [
        (passages, pas),
        (query_weight, wq),
        (table.at[pl.ds(PREFIX, TOKENS)], tail),
        (prefix, pre_v),
        (table.at[pl.ds(pl.multiple_of(px * SHARE, SHARE), SHARE)], tab),
        (kv_weight, wkv),
        (out_weight, wo),
    ]
    copies = [
        pltpu.make_async_copy(src, dst, load_sem.at[i])
        for i, (src, dst) in enumerate(loads)
    ]

    barrier = pltpu.get_barrier_semaphore()

    def greet(i, carry):
        peer = lax.rem(me + i, OWNERS)
        pl.semaphore_signal(barrier, inc=1, device_id={"corpus": peer}, device_id_type=MESH)
        return carry

    lax.fori_loop(1, OWNERS, greet, 0)
    for k in (2, 1, 3):
        pl.semaphore_signal(
            barrier, inc=1, device_id={"pre": lax.rem(px + k, PRE)}, device_id_type=MESH
        )
    for copy in copies:
        copy.start()

    def spread(source, target, channel):
        def send(i, carry):
            peer = lax.rem(me + i, OWNERS)
            pltpu.make_async_remote_copy(
                src_ref=source.at[peer],
                dst_ref=target.at[me],
                send_sem=send_sem.at[channel],
                recv_sem=recv_sem.at[channel],
                device_id={"corpus": peer},
                device_id_type=MESH,
            ).start()
            return carry

        target[me] = source[me]
        lax.fori_loop(1, OWNERS, send, 0)

    def wait_for(ref, semaphore):
        pltpu.make_async_copy(ref, ref, semaphore).wait()

    owners_c = owner_col[...]
    owners_r = owner_row[...]
    same = owners_c == owners_r
    ia = iota((SLOTS, SLOTS), 0)
    ib = iota((SLOTS, SLOTS), 1)
    rank_r = jnp.sum(jnp.where(same & (ia < ib), 1.0, 0.0), axis=0, keepdims=True)
    rank_c = jnp.sum(jnp.where(same & (ib < ia), 1.0, 0.0), axis=1, keepdims=True)
    mine = jnp.where(ia == owners_r, row_row[...].astype(F32), 0.0)
    first = jnp.sum(jnp.where(rank_r < 0.5, mine, 0.0), axis=1, keepdims=True)
    second = jnp.sum(jnp.where(rank_r > 0.5, mine, 0.0), axis=1, keepdims=True)
    lane = iota((OWNERS, 128), 1)
    message = jnp.where(lane < 8, first, second) + ((lane & 7) * PASS).astype(F32)
    req_out[...] = message.reshape(OWNERS, 1, 128)

    spot = owners_c * 16 + rank_c.astype(jnp.int32) * 8
    for j in range(8):
        place[j * SLOTS : (j + 1) * SLOTS, :] = jnp.where(
            iota((SLOTS, OWNERS * 16), 1) == spot + j, 1.0, 0.0
        ).astype(BF)

    copies[0].wait()

    def take_last(r, carry):
        start = pl.multiple_of(r * TOKENS + 16, 16)
        last32[pl.ds(r, 1), :] = pas[pl.ds(start, 16), :].astype(F32)[15:16, :]
        return carry

    lax.fori_loop(0, PASS, take_last, 0)
    last = last32[...]
    for j in range(8):
        own_rows[j * PASS : (j + 1) * PASS, :] = last[:, j * 128 : (j + 1) * 128].astype(BF)

    copies[1].wait()
    copies[2].wait()
    tail_cos, tail_sin = cos_sin(tail[...])
    end_cos, end_sin = tail_cos[TOKENS - 1 :, :], tail_sin[TOKENS - 1 :, :]

    def query_of(rows32):
        projected = dot(unit(rows32).astype(BF), wq[...])
        return [
            turn(unit(projected[:, h * HEAD : (h + 1) * HEAD]), end_cos, end_sin).astype(BF)
            for h in range(HEADS)
        ]

    for h, rows in enumerate(query_of(last)):
        own_query[h] = rows

    copies[3].wait()
    copies[4].wait()
    for half in range(2):
        span = slice(half * 256, (half + 1) * 256)
        cosine, sine = cos_sin(tab[span, :])
        for g in range(GROUPS):
            rows = pre_v[span, g * HEAD : (g + 1) * HEAD].astype(F32)
            pre_keys[g, span, :] = turn(unit(rows), cosine, sine).astype(BF)

    copies[5].wait()

    def own_chunk(c, carry):
        start = pl.multiple_of(c * CHUNK, CHUNK)
        hidden = pas[pl.ds(start, CHUNK), :]
        hidden32 = hidden.astype(F32)
        factor = lax.rsqrt(jnp.mean(hidden32 * hidden32, axis=-1, keepdims=True) + EPS)
        first_row = pl.multiple_of(c * CHUNK_PASS, CHUNK_PASS)
        cosine = jnp.broadcast_to(tail_cos[None], (CHUNK_PASS, TOKENS, HEAD)).reshape(CHUNK, HEAD)
        sine = jnp.broadcast_to(tail_sin[None], (CHUNK_PASS, TOKENS, HEAD)).reshape(CHUNK, HEAD)
        shape = (2 * CHUNK_PASS, CHUNK)
        own = (iota(shape, 0) % CHUNK_PASS) == (iota(shape, 1) // TOKENS)
        for g in range(GROUPS):
            cols = slice(g * HEAD, (g + 1) * HEAD)
            v_cols = slice((GROUPS + g) * HEAD, (GROUPS + g + 1) * HEAD)
            keys = turn(unit(dot(hidden, wkv[:, cols]) * factor), cosine, sine).astype(BF)
            values = (dot(hidden, wkv[:, v_cols]) * factor).astype(BF)
            queries = jnp.concatenate(
                [own_query[2 * g + i, pl.ds(first_row, CHUNK_PASS), :] for i in range(2)], axis=0
            )
            expo = jnp.where(own, jnp.exp(dot_t(queries, keys) * SCALE), 0.0)
            weighted = dot(expo.astype(BF), values)
            total = jnp.sum(expo, axis=1, keepdims=True)
            for i in range(2):
                rows = slice(i * CHUNK_PASS, (i + 1) * CHUNK_PASS)
                own_sums[2 * g + i, pl.ds(first_row, CHUNK_PASS), :] = weighted[rows].astype(BF)
                own_tot[2 * g + i, pl.ds(first_row, CHUNK_PASS), :] = jnp.broadcast_to(
                    total[rows], (CHUNK_PASS, HEAD)
                )
        return carry

    pl.semaphore_wait(barrier, OWNERS - 1 + PRE - 1)
    spread(req_out, req_in, 0)

    lax.fori_loop(0, PASS // CHUNK_PASS, own_chunk, 0)
    high, low = split_two(own_tot[...])
    own_tots[...] = jnp.where(iota((HEADS, PASS, HEAD), 2) < 64, high, low).astype(BF)

    wait_for(req_in.at[pl.ds(0, OWNERS - 1)], recv_sem.at[0])
    shape = (OWNERS * 16, 128)
    asked = jnp.broadcast_to(req_in[...], (OWNERS, 16, 128)).reshape(shape)
    asked = jnp.where(iota(shape, 1) == (iota(shape, 0) & 15), asked, 0.0)
    asked = jnp.sum(asked, axis=1, keepdims=True).astype(jnp.int32)
    pick[...] = jnp.where(iota((OWNERS * 16, 8 * PASS), 1) == asked, 1.0, 0.0).astype(BF)
    last_out[...] = dot(pick[...], own_rows[...]).astype(BF).reshape(OWNERS, 16, 128)
    spread(last_out, last_in, 1)
    sums_out[:, 0:16, :] = (
        dot(pick[...], own_sums[...].reshape(HEADS * PASS, HEAD)).astype(BF).reshape(OWNERS, 16, 128)
    )
    sums_out[:, 16:32, :] = (
        dot(pick[...], own_tots[...].reshape(HEADS * PASS, HEAD)).astype(BF).reshape(OWNERS, 16, 128)
    )
    spread(sums_out, sums_in, 2)

    wait_for(last_in.at[pl.ds(0, OWNERS - 1)], recv_sem.at[1])
    got = dot(place[...], last_in[...].reshape(OWNERS * 16, 128))
    slot_last[...] = jnp.concatenate(
        [got[j * SLOTS : (j + 1) * SLOTS, :] for j in range(8)], axis=1
    )
    queries = query_of(slot_last[...])
    for g in range(GROUPS):
        query_all[g, px] = jnp.concatenate([queries[2 * g], queries[2 * g + 1]], axis=0)
        for k in (2, 1, 3):
            pltpu.make_async_remote_copy(
                src_ref=query_all.at[g, px],
                dst_ref=query_all.at[g, px],
                send_sem=send_sem.at[3 + g],
                recv_sem=recv_sem.at[3 + g],
                device_id={"pre": lax.rem(px + k, PRE)},
                device_id_type=MESH,
            ).start()

    diagonal = iota((HEAD, HEAD), 0) == iota((HEAD, HEAD), 1)
    for g in range(GROUPS):
        wait_for(query_all.at[g, pl.ds(0, PRE - 1)], recv_sem.at[3 + g])
        values = pre_v[:, (GROUPS + g) * HEAD : (GROUPS + g + 1) * HEAD]
        for q in range(PRE):
            expo = jnp.exp(dot_t(query_all[g, q], pre_keys[g]) * SCALE)
            part_out[g, q, 0:HEAD, :] = dot(expo.astype(BF), values).astype(BF)
            total = jnp.sum(expo, axis=1, keepdims=True)
            total = jnp.sum(jnp.where(diagonal, total, 0.0), axis=0, keepdims=True)
            high, low = split_two(total)
            part_out[g, q, HEAD:PART, :] = jnp.where(
                iota((PART - HEAD, HEAD), 0) == 0, high, low
            ).astype(BF)
        part_in[g, px] = part_out[g, px]
        for k in (2, 1, 3):
            to = lax.rem(px + k, PRE)
            pltpu.make_async_remote_copy(
                src_ref=part_out.at[g, to],
                dst_ref=part_in.at[g, px],
                send_sem=send_sem.at[7 + g],
                recv_sem=recv_sem.at[7 + g],
                device_id={"pre": to},
                device_id_type=MESH,
            ).start()

    wait_for(sums_in.at[pl.ds(0, OWNERS - 1)], recv_sem.at[2])
    own_w = dot(place[...], sums_in[:, 0:16, :].reshape(OWNERS * 16, 128))
    own_t = dot(place[...], sums_in[:, 16:32, :].reshape(OWNERS * 16, 128))
    own_t = own_t[:, 0:1] + own_t[:, 64:65]
    copies[6].wait()
    mixed = []
    for g in range(GROUPS):
        wait_for(part_in.at[g, pl.ds(0, PRE - 1)], recv_sem.at[7 + g])
        rows = slice(g * 2 * SLOTS, (g + 1) * 2 * SLOTS)
        weighted = own_w[rows]
        total = jnp.zeros((1, HEAD), F32)
        for q in range(PRE):
            weighted = weighted + part_in[g, q, 0:HEAD, :].astype(F32)
            sums = part_in[g, q, HEAD:PART, :].astype(F32)
            total = total + sums[0:1, :] + sums[1:2, :]
        total = jnp.sum(jnp.where(diagonal, total, 0.0), axis=1, keepdims=True) + own_t[rows]
        result = (weighted / total).astype(BF)
        mixed += [result[0:SLOTS], result[SLOTS:]]
    updated = slot_last[...] + dot(jnp.concatenate(mixed, axis=1), wo[...])
    square = jnp.mean(updated * updated, axis=-1, keepdims=True)
    score = jnp.sum(updated * score_vector[...].astype(F32), axis=-1, keepdims=True)
    score = score * lax.rsqrt(square + EPS)
    score = jnp.sum(jnp.where(ia == ib, score, 0.0), axis=0, keepdims=True)
    slot = px * SLOTS + iota((1, SLOTS), 1)
    out[...] = jnp.where(slot < count[...], score, 0.0)

    wait_for(req_out.at[pl.ds(0, OWNERS - 1)], send_sem.at[0])
    wait_for(last_out.at[pl.ds(0, OWNERS - 1)], send_sem.at[1])
    wait_for(sums_out.at[pl.ds(0, OWNERS - 1)], send_sem.at[2])
    for g in range(GROUPS):
        wait_for(query_all.at[g, pl.ds(0, PRE - 1)], send_sem.at[3 + g])
        wait_for(part_out.at[g, pl.ds(0, PRE - 1)], send_sem.at[7 + g])


def per_device(
    passages,
    query_weight,
    kv_weight,
    out_weight,
    score_vector,
    prefix,
    candidate_owner,
    candidate_row,
    candidate_count,
):
    hbm = pl.BlockSpec(memory_space=pl.ANY)
    vmem = pl.BlockSpec(memory_space=pltpu.VMEM)
    return pl.pallas_call(
        kernel,
        out_shape=jax.ShapeDtypeStruct((1, SLOTS), F32),
        in_specs=[hbm, hbm, hbm, hbm, vmem, hbm, hbm, vmem, vmem, vmem, vmem],
        out_specs=vmem,
        scratch_shapes=[
            pltpu.VMEM((PASS * TOKENS, WIDTH), BF),
            pltpu.VMEM((WIDTH, WIDTH), BF),
            pltpu.VMEM((WIDTH, WIDTH), BF),
            pltpu.VMEM((WIDTH, WIDTH), BF),
            pltpu.VMEM((SHARE, WIDTH), BF),
            pltpu.VMEM((SHARE, HEAD), F32),
            pltpu.VMEM((TOKENS, HEAD), F32),
            pltpu.VMEM((PASS, WIDTH), F32),
            pltpu.VMEM((8 * PASS, 128), BF),
            pltpu.VMEM((HEADS, PASS, HEAD), BF),
            pltpu.VMEM((HEADS, PASS, HEAD), BF),
            pltpu.VMEM((HEADS, PASS, HEAD), BF),
            pltpu.VMEM((HEADS, PASS, HEAD), F32),
            pltpu.VMEM((GROUPS, SHARE, HEAD), BF),
            pltpu.VMEM((OWNERS, 1, 128), F32),
            pltpu.VMEM((OWNERS, 1, 128), F32),
            pltpu.VMEM((OWNERS * 16, 8 * PASS), BF),
            pltpu.VMEM((8 * SLOTS, OWNERS * 16), BF),
            pltpu.VMEM((OWNERS, 16, 128), BF),
            pltpu.VMEM((OWNERS, 16, 128), BF),
            pltpu.VMEM((OWNERS, 32, 128), BF),
            pltpu.VMEM((OWNERS, 32, 128), BF),
            pltpu.VMEM((GROUPS, PRE, 2 * SLOTS, HEAD), BF),
            pltpu.VMEM((GROUPS, PRE, PART, HEAD), BF),
            pltpu.VMEM((GROUPS, PRE, PART, HEAD), BF),
            pltpu.VMEM((SLOTS, WIDTH), F32),
            pltpu.SemaphoreType.DMA((7,)),
            pltpu.SemaphoreType.DMA((11,)),
            pltpu.SemaphoreType.DMA((11,)),
        ],
        compiler_params=pltpu.CompilerParams(
            collective_id=0, has_side_effects=True, vmem_limit_bytes=48 * 2**20
        ),
        cost_estimate=pl.CostEstimate(
            flops=6 * 10**9, bytes_accessed=12 * 2**20, transcendentals=2 * 10**6
        ),
    )(
        passages.reshape(PASS * TOKENS, WIDTH),
        query_weight,
        kv_weight,
        out_weight,
        score_vector.reshape(1, WIDTH),
        prefix[0],
        jnp.asarray(angle_table()),
        candidate_owner[0],
        candidate_owner.reshape(1, SLOTS),
        candidate_row,
        candidate_count.reshape(1, 1),
    )


def solution(mesh):
    return jax.shard_map(
        per_device,
        mesh=mesh,
        in_specs=(
            P("corpus", None, None),
            P(),
            P(),
            P(),
            P(),
            P("corpus", "pre", None),
            P("corpus", "pre", None),
            P("corpus", "pre"),
            P("corpus"),
        ),
        out_specs=P("corpus", "pre"),
        check_vma=False,
    )
```

time: 299 us -> 65.1 us (0.22)
  waiting for transfers between devices: 157 us -> 0 us
  Pallas kernels: 0 us -> 56.9 us
  local copies, waits for them, and re-layouts: 46.3 us -> 7.3 us
  other arithmetic: 32.1 us -> 0 us
  blocking collectives: 22.3 us -> 0 us
  matrix products: 17.5 us -> 0 us
  between operations: 14.5 us -> 0.67 us
  starting transfers between devices: 6.16 us -> 0 us
    all_to_all x1 -> x0, waiting for transfers between devices: 111 us -> none  [per_device(): lax.all_to_all(served.reshape(peer_count, capacity, prefix_length, width)...]
    pallas_call x0 -> x1, Pallas kernels: none -> 56.9 us  [per_device(): pl.pallas_call(kernel, out_shape=jax.ShapeDtypeStruct((1, SLOTS), F32), i...]
    all_gather x1 -> x0, waiting for transfers between devices: 46.6 us -> none  [per_device(): lax.all_gather(prefix_key_value_state, 'pre', axis=1, tiled=True)[0]]
    all_to_all x1 -> x0, blocking collectives: 22.3 us -> none  [per_device(): lax.all_to_all(request, 'corpus', split_axis=0, concat_axis=0, tiled=True)]
    dot_general x7 -> x0, matrix products: 17.5 us -> none  [the longest x1 6.38 us: passage_states(): jnp.dot(normed.reshape(row_tally * prefix_length, hidden.shape[2]), kv_we...]
    gather x2 -> x0, local copies, waits for them, and re-layouts: 14.7 us -> none  [the longest x1 8.56 us: per_device(): served = passages[arrived.reshape(-1)]]
    slice x3 -> x0, local copies, waits for them, and re-layouts: 11.3 us -> none  [the longest x1 4.84 us: prefix_terms(): block_slice[:, :KEY_VALUE_HEADS * HEAD_SIZE].astype(jnp.float32)]
    reduce_sum x7 -> x0, other arithmetic: 11.2 us -> none  [the longest x5 10.1 us: rms_rows(): jnp.mean(value_rows * value_rows, axis=-1, keepdims=True) + epsilon]
  transfers between devices with their start and end apart: 2 -> 0, of which waited for: 2 -> 0; matrix products, arithmetic and copies ran while one was open for 8% -> 0% of each run, Pallas kernels for 0% -> 0%
where the time goes in v1:
time: 65.1 us; the launch traced here: 64.9 us
  Pallas kernels  56.9 us (87%)
  local copies, waits for them, and re-layouts  7.3 us (11%)
  between operations  0.67 us (1%)
    pallas_call x1, Pallas kernels, per_device(): pl.pallas_call(kernel, out_shape=jax.ShapeDtypeStruct((1, SLOTS), F32), i...  56.9 us
    unnamed x11, local copies, waits for them, and re-layouts  5.87 us

profile of v1, /device:TPU:1, one launch (start us, length us, event | category | flops | bytes accessed | tf_op | source)
XLA Modules:
  0.0 64.9 jit_solution(5930042432796331560)
XLA Ops:
  0.7 0.7 %reshape.13.score_vector = bf16[1,1024]{1,0:T(2,128)(2,1)S(1)} reshape(bf16[1024]{0:T(1024)(128)(2,1)} %param.14) | data formatting | bytes 4096 | tf_op jit(solution)/shard_map/reshape | solution.py:378
  1.3 0.7 %copy.11.owner_col = s32[64,1]{1,0:T(8,128)S(1)} copy(s32[64,1]{0,1:T(1,128)} %bitcast.6) | data formatting | bytes 512 | tf_op jit(solution)/shard_map/squeeze | solution.py:381
  2.1 0.0 copy-start
  2.1 0.7 %copy-done = s32[1,64,1]{1,2,0:T(1,128)S(1)} copy-done((s32[1,64,1]{1,2,0:T(1,128)S(1)}, s32[1,64,1]{1,2,0:T(1,128)}, u32[]{:S(2)}) %copy-start) | copy-done | bytes 280
  2.7 0.0 copy-start.1
  2.7 1.6 %copy-done.1 = bf16[1024,1024]{1,0:T(8,128)(2,1)S(1)} copy-done((bf16[1024,1024]{1,0:T(8,128)(2,1)S(1)}, bf16[1024,1024]{1,0:T(8,128)(2,1)}, u32[]{:S(2)}) %copy-start.1) | copy-done | bytes 2097176
  4.3 0.0 copy-start.2
  4.3 1.2 %copy-done.2 = bf16[1,512,1024]{2,1,0:T(8,128)(2,1)S(1)} copy-done((bf16[1,512,1024]{2,1,0:T(8,128)(2,1)S(1)}, bf16[1,512,1024]{2,1,0:T(8,128)(2,1)}, u32[]{:S(2)}) %copy-start.2) | copy-done | bytes 1048600
  5.6 0.0 copy-start.3
  5.6 0.7 %copy-done.3 = s32[1,64]{1,0:T(1,128)S(1)} copy-done((s32[1,64]{1,0:T(1,128)S(1)}, s32[1,64]{1,0:T(1,128)}, u32[]{:S(2)}) %copy-start.3) | copy-done | bytes 280
  6.2 0.0 copy-start.4
  6.2 1.2 %copy-done.4 = f32[2080,128]{1,0:T(8,128)S(1)} copy-done((f32[2080,128]{1,0:T(8,128)S(1)}, f32[2080,128]{1,0:T(8,128)}, u32[]{:S(2)}) %copy-start.4) | copy-done | bytes 1064984
  7.4 56.9 %shard_map.100 = f32[1,64]{1,0:T(1,128)S(1)} custom-call(bf16[2048,1024]{1,0:T(8,128)(2,1)} %bitcast.9, bf16[1024,1024]{1,0:T(8,128)(2,1)S(1)} %copy-done.1, bf16[1024,1024]{1,0:T(8,128)(2,1)} %kv_weight.1, bf16[1024,1024]{1,0:T(8,128)(2,1)} %out_weight.1, bf16[1,1024]{1,0:T(2,128)(2,1)S(1)} %reshape.13.score_vector, bf16[512,1024]{1,0:T(8,128)(2,1)S(1)} %bitcast.8, ...), custom_call_target="tpu_custom_call" | custom-call | flops 6000000000 | bytes 12582912 | tf_op jit(solution)/shard_map/pallas_call | solution.py:331
  64.4 0.5 copy.14
Async XLA Ops:
  2.1 0.7 %copy-start = (s32[1,64,1]{1,2,0:T(1,128)S(1)}, s32[1,64,1]{1,2,0:T(1,128)}, u32[]{:S(2)}) copy-start(s32[1,64,1]{1,2,0:T(1,128)} %param.16) | copy-start | bytes 772
  2.7 1.6 %copy-start.1 = (bf16[1024,1024]{1,0:T(8,128)(2,1)S(1)}, bf16[1024,1024]{1,0:T(8,128)(2,1)}, u32[]{:S(2)}) copy-start(bf16[1024,1024]{1,0:T(8,128)(2,1)} %query_weight.1) | copy-start | bytes 6291460
  4.3 1.2 %copy-start.2 = (bf16[1,512,1024]{2,1,0:T(8,128)(2,1)S(1)}, bf16[1,512,1024]{2,1,0:T(8,128)(2,1)}, u32[]{:S(2)}) copy-start(bf16[1,512,1024]{2,1,0:T(8,128)(2,1)} %param.15) | copy-start | bytes 3145732
  5.6 0.7 %copy-start.3 = (s32[1,64]{1,0:T(1,128)S(1)}, s32[1,64]{1,0:T(1,128)}, u32[]{:S(2)}) copy-start(s32[1,64]{1,0:T(1,128)} %row_row.1) | copy-start | bytes 772
  6.2 1.2 %copy-start.4 = (f32[2080,128]{1,0:T(8,128)S(1)}, f32[2080,128]{1,0:T(8,128)}, u32[]{:S(2)}) copy-start(f32[2080,128]{1,0:T(8,128)} %constant.2.clone.table) | copy-start | bytes 3194884

commit v2 on v1

v2 whole, which is shorter than its diff:
```python
import jax
import jax.numpy as jnp
import numpy as np
from jax import lax
from jax.experimental import pallas as pl
from jax.experimental.pallas import tpu as pltpu
from jax.sharding import PartitionSpec as P

MESH = pl.DeviceIdType.MESH
BF = jnp.bfloat16
F32 = jnp.float32

OWNERS = 64
PRE = 4
SLOTS = 64
PASS = 64
TOKENS = 32
WIDTH = 1024
HEADS = 8
GROUPS = 4
HEAD = 128
PREFIX = 2048
SHARE = PREFIX // PRE
CHUNK = 512
SCALE = HEAD**-0.5
EPS = 1e-06
PART = HEAD + 16
VLIM = 62
BLOCK = PASS // PRE
WHOLE = 1


def angle_table():
    half = HEAD // 2
    exponent = np.arange(half, dtype=np.float32) * np.float32(2.0 / HEAD)
    freq = np.float32(1000000.0) ** (-exponent)
    angles = np.arange(PREFIX + TOKENS, dtype=np.float32)[:, None] * freq[None, :]
    angles = angles.astype(np.float64)
    return np.concatenate([np.cos(angles), np.sin(angles)], axis=1).astype(np.float32)


def iota(shape, dim):
    return lax.broadcasted_iota(jnp.int32, shape, dim)


def cos_sin(table):
    swapped = pltpu.roll(table, HEAD // 2, 1)
    low = iota(table.shape, 1) < HEAD // 2
    return jnp.where(low, table, swapped), jnp.where(low, -swapped, table)


def unit(rows):
    return rows * lax.rsqrt(jnp.mean(rows * rows, axis=-1, keepdims=True) + EPS)


def turn(rows, cosine, sine):
    return rows * cosine + pltpu.roll(rows, HEAD // 2, 1) * sine


def dot(a, b):
    return jnp.dot(a, b, preferred_element_type=F32)


def dot_t(a, b):
    return lax.dot_general(a, b, (((1,), (1,)), ((), ())), preferred_element_type=F32)


def split_two(total):
    high = total.astype(BF).astype(F32)
    return high, total - high


def kernel(
    passages, query_weight, kv_weight, out_weight, score_vector, prefix, table,
    owner, row, count, out,
    pas, ends, wq, wkv, wo, pre_v, tab, tail,
    last32, own_rows, own_share, heads_all, pre_keys, req_out, req_in, pick, place,
    last_out, last_in, sums_out, sums_in, query_all, part_out, part_in, slot_last,
    owner_row, row_row, score_v, load_sem, send_sem, recv_sem,
):
    me = lax.axis_index("corpus")
    px = lax.axis_index("pre")

    loads = [
        (owner, owner_row),
        (row, row_row),
        (passages.at[:, pl.ds(16, 16)], ends),
        (query_weight, wq),
        (table.at[pl.ds(PREFIX, TOKENS)], tail),
        (prefix, pre_v),
        (table.at[pl.ds(pl.multiple_of(px * SHARE, SHARE), SHARE)], tab),
        (passages.at[pl.ds(pl.multiple_of(px * BLOCK, BLOCK), BLOCK)], pas),
        (kv_weight, wkv),
        (out_weight, wo),
        (score_vector, score_v),
    ]
    copies = [
        pltpu.make_async_copy(src, dst, load_sem.at[i])
        for i, (src, dst) in enumerate(loads)
    ]

    barrier = pltpu.get_barrier_semaphore()

    def greet(i, carry):
        peer = lax.rem(me + i, OWNERS)
        pl.semaphore_signal(barrier, inc=1, device_id={"corpus": peer}, device_id_type=MESH)
        return carry

    lax.fori_loop(1, OWNERS, greet, 0)
    for k in (2, 1, 3):
        pl.semaphore_signal(
            barrier, inc=1, device_id={"pre": lax.rem(px + k, PRE)}, device_id_type=MESH
        )
    for copy in copies:
        copy.start()

    def spread(source, target, channel):
        def send(i, carry):
            peer = lax.rem(me + i, OWNERS)
            pltpu.make_async_remote_copy(
                src_ref=source.at[peer],
                dst_ref=target.at[me],
                send_sem=send_sem.at[channel],
                recv_sem=recv_sem.at[channel],
                device_id={"corpus": peer},
                device_id_type=MESH,
            ).start()
            return carry

        target[me] = source[me]
        lax.fori_loop(1, OWNERS, send, 0)

    def wait_for(ref, semaphore):
        pltpu.make_async_copy(ref, ref, semaphore).wait()

    copies[0].wait()
    copies[1].wait()
    ia = iota((SLOTS, SLOTS), 0)
    ib = iota((SLOTS, SLOTS), 1)
    owners_r = owner_row[...]
    owners_c = jnp.sum(jnp.where(ia == ib, owners_r.astype(F32), 0.0), axis=1, keepdims=True)
    owners_c = owners_c.astype(jnp.int32)
    same = owners_c == owners_r
    rank_r = jnp.sum(jnp.where(same & (ia < ib), 1.0, 0.0), axis=0, keepdims=True)
    rank_c = jnp.sum(jnp.where(same & (ib < ia), 1.0, 0.0), axis=1, keepdims=True)
    mine = jnp.where(ia == owners_r, row_row[...].astype(F32), 0.0)
    first = jnp.sum(jnp.where(rank_r < 0.5, mine, 0.0), axis=1, keepdims=True)
    second = jnp.sum(jnp.where(rank_r > 0.5, mine, 0.0), axis=1, keepdims=True)
    lane = iota((OWNERS, 128), 1)
    wanted = jnp.where(lane < 8, first, second).astype(jnp.int32)
    wanted = (wanted // BLOCK) * (8 * BLOCK) + (lane & 7) * BLOCK + wanted % BLOCK
    req_out[...] = wanted.astype(F32).reshape(OWNERS, 1, 128)

    spot = owners_c * 16 + rank_c.astype(jnp.int32) * 8
    for j in range(8):
        place[j * SLOTS : (j + 1) * SLOTS, :] = jnp.where(
            iota((SLOTS, OWNERS * 16), 1) == spot + j, 1.0, 0.0
        ).astype(BF)

    copies[2].wait()

    def take_last(r, carry):
        last32[pl.ds(r, 1), :] = ends[r].astype(F32)[15:16, :]
        return carry

    lax.fori_loop(0, PASS, take_last, 0)
    last = last32[...].astype(BF)
    for q in range(PRE):
        for j in range(8):
            start = (q * 8 + j) * BLOCK
            own_rows[start : start + BLOCK, :] = last[
                q * BLOCK : (q + 1) * BLOCK, j * 128 : (j + 1) * 128
            ]

    copies[3].wait()
    copies[4].wait()
    tail_cos, tail_sin = cos_sin(tail[...])
    end_cos, end_sin = tail_cos[TOKENS - 1 :, :], tail_sin[TOKENS - 1 :, :]

    def query_of(normed, g):
        projected = dot(normed, wq[:, 2 * g * HEAD : 2 * (g + 1) * HEAD])
        parts = [
            turn(unit(projected[:, i * HEAD : (i + 1) * HEAD]), end_cos, end_sin).astype(BF)
            for i in range(2)
        ]
        return jnp.concatenate(parts, axis=0)

    copies[5].wait()
    copies[6].wait()
    for half in range(2):
        span = slice(half * 256, (half + 1) * 256)
        cosine, sine = cos_sin(tab[span, :])
        for g in range(GROUPS):
            rows = pre_v[span, g * HEAD : (g + 1) * HEAD].astype(F32)
            keys = turn(unit(rows), cosine, sine).astype(BF)
            if g < WHOLE:
                heads_all[g, px, 0, span, :] = keys
                heads_all[g, px, 1, span, :] = pre_v[
                    span, (GROUPS + g) * HEAD : (GROUPS + g + 1) * HEAD
                ]
            else:
                pre_keys[g, span, :] = keys

    copies[7].wait()
    copies[8].wait()
    hidden = pas[...].reshape(CHUNK, WIDTH)
    hidden32 = hidden.astype(F32)
    factor = lax.rsqrt(jnp.mean(hidden32 * hidden32, axis=-1, keepdims=True) + EPS)
    cosine = jnp.broadcast_to(tail_cos[None], (BLOCK, TOKENS, HEAD)).reshape(CHUNK, HEAD)
    sine = jnp.broadcast_to(tail_sin[None], (BLOCK, TOKENS, HEAD)).reshape(CHUNK, HEAD)
    shape = (2 * BLOCK, CHUNK)
    own = (iota(shape, 0) % BLOCK) == (iota(shape, 1) // TOKENS)
    normed = unit(last32[pl.ds(pl.multiple_of(px * BLOCK, BLOCK), BLOCK), :]).astype(BF)
    for pair in range(GROUPS // 2):
        cols = slice(2 * pair * HEAD, 2 * (pair + 1) * HEAD)
        v_cols = slice((GROUPS + 2 * pair) * HEAD, (GROUPS + 2 * (pair + 1)) * HEAD)
        both_keys = dot(hidden, wkv[:, cols]) * factor
        both_values = (dot(hidden, wkv[:, v_cols]) * factor).astype(BF)
        for i in range(2):
            g = 2 * pair + i
            keys = turn(unit(both_keys[:, i * HEAD : (i + 1) * HEAD]), cosine, sine).astype(BF)
            values = both_values[:, i * HEAD : (i + 1) * HEAD]
            expo = jnp.where(own, jnp.exp(dot_t(query_of(normed, g), keys) * SCALE), 0.0)
            weighted = dot(expo.astype(BF), values).astype(BF)
            high, low = split_two(jnp.sum(expo, axis=1, keepdims=True))
            total = jnp.where(iota((2 * BLOCK, HEAD), 1) < 64, high, low).astype(BF)
            for h in range(2):
                rows = slice(h * BLOCK, (h + 1) * BLOCK)
                own_share[px, 0, 2 * g + h] = weighted[rows]
                own_share[px, 1, 2 * g + h] = total[rows]

    def to_row(ref, channel):
        for k in (2, 1, 3):
            to = lax.rem(px + k, PRE)
            pltpu.make_async_remote_copy(
                src_ref=ref.at[px],
                dst_ref=ref.at[px],
                send_sem=send_sem.at[channel],
                recv_sem=recv_sem.at[channel],
                device_id={"pre": to},
                device_id_type=MESH,
            ).start()

    pl.semaphore_wait(barrier, OWNERS - 1 + PRE - 1)
    spread(req_out, req_in, 0)
    to_row(own_share, 3)
    for g in range(WHOLE):
        to_row(heads_all.at[g], 4 + g)

    wait_for(req_in.at[pl.ds(0, OWNERS - 1)], recv_sem.at[0])
    shape = (OWNERS * 16, 128)
    asked = jnp.broadcast_to(req_in[...], (OWNERS, 16, 128)).reshape(shape)
    asked = jnp.where(iota(shape, 1) == (iota(shape, 0) & 15), asked, 0.0)
    asked = jnp.sum(asked, axis=1, keepdims=True).astype(jnp.int32)
    pick[...] = jnp.where(iota((OWNERS * 16, 8 * PASS), 1) == asked, 1.0, 0.0).astype(BF)
    last_out[...] = dot(pick[...], own_rows[...]).astype(BF).reshape(OWNERS, 16, 128)
    spread(last_out, last_in, 1)
    wait_for(own_share.at[pl.ds(0, PRE - 1)], recv_sem.at[3])
    for i in range(2):
        served = dot(pick[...], own_share[:, i].reshape(HEADS * PASS, HEAD)).astype(BF)
        sums_out[:, i * 16 : (i + 1) * 16, :] = served.reshape(OWNERS, 16, 128)
    spread(sums_out, sums_in, 2)

    wait_for(last_in.at[pl.ds(0, OWNERS - 1)], recv_sem.at[1])
    got = dot(place[...], last_in[...].reshape(OWNERS * 16, 128))
    slot_last[...] = jnp.concatenate(
        [got[j * SLOTS : (j + 1) * SLOTS, :] for j in range(8)], axis=1
    )
    normed = unit(slot_last[...]).astype(BF)
    for g in (*range(WHOLE, GROUPS), *range(WHOLE)):
        query_all[g, px] = query_of(normed, g)
        if g >= WHOLE:
            to_row(query_all.at[g], 4 + g)

    diagonal = iota((HEAD, HEAD), 0) == iota((HEAD, HEAD), 1)
    whole = []
    for g in range(WHOLE):
        wait_for(heads_all.at[g, pl.ds(0, PRE - 1)], recv_sem.at[4 + g])
        weighted = jnp.zeros((2 * SLOTS, HEAD), F32)
        total = jnp.zeros((2 * SLOTS, 1), F32)
        for q in range(PRE):
            expo = jnp.exp(dot_t(query_all[g, px], heads_all[g, q, 0]) * SCALE)
            weighted = weighted + dot(expo.astype(BF), heads_all[g, q, 1])
            total = total + jnp.sum(expo, axis=1, keepdims=True)
        whole.append((weighted, total))
    for g in range(WHOLE, GROUPS):
        wait_for(query_all.at[g, pl.ds(0, PRE - 1)], recv_sem.at[4 + g])
        values = pre_v[:, (GROUPS + g) * HEAD : (GROUPS + g + 1) * HEAD]
        for q in range(PRE):
            expo = jnp.exp(dot_t(query_all[g, q], pre_keys[g]) * SCALE)
            part_out[g, q, 0:HEAD, :] = dot(expo.astype(BF), values).astype(BF)
            total = jnp.sum(expo, axis=1, keepdims=True)
            total = jnp.sum(jnp.where(diagonal, total, 0.0), axis=0, keepdims=True)
            high, low = split_two(total)
            part_out[g, q, HEAD:PART, :] = jnp.where(
                iota((PART - HEAD, HEAD), 0) == 0, high, low
            ).astype(BF)
        part_in[g, px] = part_out[g, px]
        for k in (2, 1, 3):
            to = lax.rem(px + k, PRE)
            pltpu.make_async_remote_copy(
                src_ref=part_out.at[g, to],
                dst_ref=part_in.at[g, px],
                send_sem=send_sem.at[8 + g],
                recv_sem=recv_sem.at[8 + g],
                device_id={"pre": to},
                device_id_type=MESH,
            ).start()

    wait_for(sums_in.at[pl.ds(0, OWNERS - 1)], recv_sem.at[2])
    own_w = dot(place[...], sums_in[:, 0:16, :].reshape(OWNERS * 16, 128))
    own_t = dot(place[...], sums_in[:, 16:32, :].reshape(OWNERS * 16, 128))
    own_t = own_t[:, 0:1] + own_t[:, 64:65]
    copies[9].wait()
    copies[10].wait()
    mixed = []
    for g in range(GROUPS):
        rows = slice(g * 2 * SLOTS, (g + 1) * 2 * SLOTS)
        if g < WHOLE:
            weighted, total = whole[g]
            weighted = weighted + own_w[rows]
        else:
            wait_for(part_in.at[g, pl.ds(0, PRE - 1)], recv_sem.at[8 + g])
            weighted = own_w[rows]
            total = jnp.zeros((1, HEAD), F32)
            for q in range(PRE):
                weighted = weighted + part_in[g, q, 0:HEAD, :].astype(F32)
                sums = part_in[g, q, HEAD:PART, :].astype(F32)
                total = total + sums[0:1, :] + sums[1:2, :]
            total = jnp.sum(jnp.where(diagonal, total, 0.0), axis=1, keepdims=True)
        total = total + own_t[rows]
        result = (weighted / total).astype(BF)
        mixed += [result[0:SLOTS], result[SLOTS:]]
    updated = slot_last[...] + dot(jnp.concatenate(mixed, axis=1), wo[...])
    square = jnp.mean(updated * updated, axis=-1, keepdims=True)
    weights = score_v[...].astype(F32)
    weights = jnp.concatenate([weights[j : j + 1, :] for j in range(8)], axis=1)
    score = jnp.sum(updated * weights, axis=-1, keepdims=True)
    score = score * lax.rsqrt(square + EPS)
    score = jnp.sum(jnp.where(ia == ib, score, 0.0), axis=0, keepdims=True)
    slot = px * SLOTS + iota((1, SLOTS), 1)
    out[...] = jnp.where(slot < count[0], score, 0.0)

    wait_for(req_out.at[pl.ds(0, OWNERS - 1)], send_sem.at[0])
    wait_for(last_out.at[pl.ds(0, OWNERS - 1)], send_sem.at[1])
    wait_for(sums_out.at[pl.ds(0, OWNERS - 1)], send_sem.at[2])
    wait_for(own_share.at[pl.ds(0, PRE - 1)], send_sem.at[3])
    for g in range(WHOLE):
        wait_for(heads_all.at[g, pl.ds(0, PRE - 1)], send_sem.at[4 + g])
    for g in range(WHOLE, GROUPS):
        wait_for(query_all.at[g, pl.ds(0, PRE - 1)], send_sem.at[4 + g])
        wait_for(part_out.at[g, pl.ds(0, PRE - 1)], send_sem.at[8 + g])


def per_device(
    passages,
    query_weight,
    kv_weight,
    out_weight,
    score_vector,
    prefix,
    candidate_owner,
    candidate_row,
    candidate_count,
):
    hbm = pl.BlockSpec(memory_space=pl.ANY)
    return pl.pallas_call(
        kernel,
        out_shape=jax.ShapeDtypeStruct((1, SLOTS), F32),
        in_specs=[hbm] * 9 + [pl.BlockSpec(memory_space=pltpu.SMEM)],
        out_specs=pl.BlockSpec(memory_space=pltpu.VMEM),
        scratch_shapes=[
            pltpu.VMEM((BLOCK, TOKENS, WIDTH), BF),
            pltpu.VMEM((PASS, 16, WIDTH), BF),
            pltpu.VMEM((WIDTH, WIDTH), BF),
            pltpu.VMEM((WIDTH, WIDTH), BF),
            pltpu.VMEM((WIDTH, WIDTH), BF),
            pltpu.VMEM((SHARE, WIDTH), BF),
            pltpu.VMEM((SHARE, HEAD), F32),
            pltpu.VMEM((TOKENS, HEAD), F32),
            pltpu.VMEM((PASS, WIDTH), F32),
            pltpu.VMEM((8 * PASS, 128), BF),
            pltpu.VMEM((PRE, 2, HEADS, BLOCK, HEAD), BF),
            pltpu.VMEM((max(WHOLE, 1), PRE, 2, SHARE, HEAD), BF),
            pltpu.VMEM((GROUPS, SHARE, HEAD), BF),
            pltpu.VMEM((OWNERS, 1, 128), F32),
            pltpu.VMEM((OWNERS, 1, 128), F32),
            pltpu.VMEM((OWNERS * 16, 8 * PASS), BF),
            pltpu.VMEM((8 * SLOTS, OWNERS * 16), BF),
            pltpu.VMEM((OWNERS, 16, 128), BF),
            pltpu.VMEM((OWNERS, 16, 128), BF),
            pltpu.VMEM((OWNERS, 32, 128), BF),
            pltpu.VMEM((OWNERS, 32, 128), BF),
            pltpu.VMEM((GROUPS, PRE, 2 * SLOTS, HEAD), BF),
            pltpu.VMEM((GROUPS, PRE, PART, HEAD), BF),
            pltpu.VMEM((GROUPS, PRE, PART, HEAD), BF),
            pltpu.VMEM((SLOTS, WIDTH), F32),
            pltpu.VMEM((1, SLOTS), jnp.int32),
            pltpu.VMEM((1, SLOTS), jnp.int32),
            pltpu.VMEM((8, 128), BF),
            pltpu.SemaphoreType.DMA((11,)),
            pltpu.SemaphoreType.DMA((12,)),
            pltpu.SemaphoreType.DMA((12,)),
        ],
        compiler_params=pltpu.CompilerParams(
            collective_id=0, has_side_effects=True, vmem_limit_bytes=VLIM * 2**20
        ),
        cost_estimate=pl.CostEstimate(
            flops=6 * 10**9, bytes_accessed=12 * 2**20, transcendentals=2 * 10**6
        ),
    )(
        passages,
        query_weight,
        kv_weight,
        out_weight,
        score_vector.reshape(8, 128),
        prefix[0],
        jnp.asarray(angle_table()),
        candidate_owner.reshape(1, SLOTS),
        candidate_row,
        candidate_count,
    )


def solution(mesh):
    return jax.shard_map(
        per_device,
        mesh=mesh,
        in_specs=(
            P("corpus", None, None),
            P(),
            P(),
            P(),
            P(),
            P("corpus", "pre", None),
            P("corpus", "pre", None),
            P("corpus", "pre"),
            P("corpus"),
        ),
        out_specs=P("corpus", "pre"),
        check_vma=False,
    )
```

time: 65.1 us -> 48.8 us (0.75); the launches traced: 64.9 us -> 47.9 us
  Pallas kernels: 56.9 us -> 46 us
  local copies, waits for them, and re-layouts: 7.3 us -> 1.19 us
    pallas_call x1, Pallas kernels: 56.9 us -> 46 us  [per_device(): pl.pallas_call(kernel, out_shape=jax.ShapeDtypeStruct((1, SLOTS), F32), i...]
    unnamed x11 -> x1, local copies, waits for them, and re-layouts: 5.87 us -> 1.19 us
    squeeze x1 -> x0, local copies, waits for them, and re-layouts: 0.74 us -> none  [per_device(): candidate_owner[0]]
    reshape x1 -> x0, local copies, waits for them, and re-layouts: 0.69 us -> none  [per_device(): score_vector.reshape(1, WIDTH)]
where the time goes in v2:
time: 48.8 us; the launch traced here: 47.9 us
  Pallas kernels  46 us (94%)
  local copies, waits for them, and re-layouts  1.19 us (2%)
  between operations  0.66 us (1%)
    pallas_call x1, Pallas kernels, per_device(): pl.pallas_call(kernel, out_shape=jax.ShapeDtypeStruct((1, SLOTS), F32), i...  46 us
    unnamed x1, local copies, waits for them, and re-layouts  1.19 us

profile of v2, /device:TPU:1, one launch (start us, length us, event | category | flops | bytes accessed | tf_op | source)
XLA Modules:
  0.0 47.9 jit_solution(17045093451398342920)
XLA Ops:
  0.7 46.0 %shard_map.100 = f32[1,64]{1,0:T(1,128)} custom-call(bf16[64,32,1024]{2,1,0:T(8,128)(2,1)} %passages.1, bf16[1024,1024]{1,0:T(8,128)(2,1)} %query_weight.1, bf16[1024,1024]{1,0:T(8,128)(2,1)} %kv_weight.1, bf16[1024,1024]{1,0:T(8,128)(2,1)} %out_weight.1, bf16[8,128]{1,0:T(8,128)(2,1)} %bitcast.4, bf16[512,1024]{1,0:T(8,128)(2,1)} %bitcast.3, ...), custom_call_target="tpu_custom_call" | custom-call | flops 6000000000 | bytes 12582912 | tf_op jit(solution)/shard_map/pallas_call | solution.py:367
  46.7 1.2 %copy.13 = f32[1,64]{1,0:T(1,128)} copy(f32[1,64]{1,0:T(1,128)} %shard_map.100) | data formatting | bytes 512

commit v3 on v2

--- a/solution.py
+++ b/solution.py
@@ -185,22 +185,42 @@
         ]
         return jnp.concatenate(parts, axis=0)
 
+    def to_row(ref, channel, at=()):
+        for k in (2, 1, 3):
+            to = lax.rem(px + k, PRE)
+            pltpu.make_async_remote_copy(
+                src_ref=ref.at[(px, *at)],
+                dst_ref=ref.at[(px, *at)],
+                send_sem=send_sem.at[channel],
+                recv_sem=recv_sem.at[channel],
+                device_id={"pre": to},
+                device_id_type=MESH,
+            ).start()
+
     copies[5].wait()
     copies[6].wait()
-    for half in range(2):
-        span = slice(half * 256, (half + 1) * 256)
-        cosine, sine = cos_sin(tab[span, :])
-        for g in range(GROUPS):
-            rows = pre_v[span, g * HEAD : (g + 1) * HEAD].astype(F32)
-            keys = turn(unit(rows), cosine, sine).astype(BF)
-            if g < WHOLE:
-                heads_all[g, px, 0, span, :] = keys
-                heads_all[g, px, 1, span, :] = pre_v[
-                    span, (GROUPS + g) * HEAD : (GROUPS + g + 1) * HEAD
-                ]
-            else:
-                pre_keys[g, span, :] = keys
-
+
+    def prefix_keys(heads):
+        for half in range(2):
+            span = slice(half * 256, (half + 1) * 256)
+            cosine, sine = cos_sin(tab[span, :])
+            for g in heads:
+                rows = pre_v[span, g * HEAD : (g + 1) * HEAD].astype(F32)
+                keys = turn(unit(rows), cosine, sine).astype(BF)
+                if g < WHOLE:
+                    heads_all[g, px, 0, span, :] = keys
+                    heads_all[g, px, 1, span, :] = pre_v[
+                        span, (GROUPS + g) * HEAD : (GROUPS + g + 1) * HEAD
+                    ]
+                else:
+                    pre_keys[g, span, :] = keys
+
+    prefix_keys(range(WHOLE))
+
+    pl.semaphore_wait(barrier, OWNERS - 1 + PRE - 1)
+    for g in range(WHOLE):
+        to_row(heads_all.at[g], 4 + g, (0,))
+    spread(req_out, req_in, 0)
     copies[7].wait()
     copies[8].wait()
     hidden = pas[...].reshape(CHUNK, WIDTH)
@@ -229,23 +249,9 @@
                 own_share[px, 0, 2 * g + h] = weighted[rows]
                 own_share[px, 1, 2 * g + h] = total[rows]
 
-    def to_row(ref, channel):
-        for k in (2, 1, 3):
-            to = lax.rem(px + k, PRE)
-            pltpu.make_async_remote_copy(
-                src_ref=ref.at[px],
-                dst_ref=ref.at[px],
-                send_sem=send_sem.at[channel],
-                recv_sem=recv_sem.at[channel],
-                device_id={"pre": to},
-                device_id_type=MESH,
-            ).start()
-
-    pl.semaphore_wait(barrier, OWNERS - 1 + PRE - 1)
-    spread(req_out, req_in, 0)
     to_row(own_share, 3)
     for g in range(WHOLE):
-        to_row(heads_all.at[g], 4 + g)
+        to_row(heads_all.at[g], 8 + g, (1,))
 
     wait_for(req_in.at[pl.ds(0, OWNERS - 1)], recv_sem.at[0])
     shape = (OWNERS * 16, 128)
@@ -255,6 +261,7 @@
     pick[...] = jnp.where(iota((OWNERS * 16, 8 * PASS), 1) == asked, 1.0, 0.0).astype(BF)
     last_out[...] = dot(pick[...], own_rows[...]).astype(BF).reshape(OWNERS, 16, 128)
     spread(last_out, last_in, 1)
+    prefix_keys(range(WHOLE, GROUPS))
     wait_for(own_share.at[pl.ds(0, PRE - 1)], recv_sem.at[3])
     for i in range(2):
         served = dot(pick[...], own_share[:, i].reshape(HEADS * PASS, HEAD)).astype(BF)
@@ -275,7 +282,8 @@
     diagonal = iota((HEAD, HEAD), 0) == iota((HEAD, HEAD), 1)
     whole = []
     for g in range(WHOLE):
-        wait_for(heads_all.at[g, pl.ds(0, PRE - 1)], recv_sem.at[4 + g])
+        wait_for(heads_all.at[g, pl.ds(0, PRE - 1), 0], recv_sem.at[4 + g])
+        wait_for(heads_all.at[g, pl.ds(0, PRE - 1), 1], recv_sem.at[8 + g])
         weighted = jnp.zeros((2 * SLOTS, HEAD), F32)
         total = jnp.zeros((2 * SLOTS, 1), F32)
         for q in range(PRE):
@@ -346,7 +354,8 @@
     wait_for(sums_out.at[pl.ds(0, OWNERS - 1)], send_sem.at[2])
     wait_for(own_share.at[pl.ds(0, PRE - 1)], send_sem.at[3])
     for g in range(WHOLE):
-        wait_for(heads_all.at[g, pl.ds(0, PRE - 1)], send_sem.at[4 + g])
+        wait_for(heads_all.at[g, pl.ds(0, PRE - 1), 0], send_sem.at[4 + g])
+        wait_for(heads_all.at[g, pl.ds(0, PRE - 1), 1], send_sem.at[8 + g])
     for g in range(WHOLE, GROUPS):
         wait_for(query_all.at[g, pl.ds(0, PRE - 1)], send_sem.at[4 + g])
         wait_for(part_out.at[g, pl.ds(0, PRE - 1)], send_sem.at[8 + g])

time: 48.8 us -> 44.7 us (0.916); the launches traced: 47.9 us -> 44.6 us
  Pallas kernels: 46 us -> 42.8 us
    pallas_call x1, Pallas kernels: 46 us -> 42.8 us  [per_device(): pl.pallas_call(kernel, out_shape=jax.ShapeDtypeStruct((1, SLOTS), F32), i...]
where the time goes in v3:
time: 44.7 us; the launch traced here: 44.6 us
  Pallas kernels  42.8 us (96%)
  local copies, waits for them, and re-layouts  1.19 us (3%)
  between operations  0.66 us (1%)
    pallas_call x1, Pallas kernels, per_device(): pl.pallas_call(kernel, out_shape=jax.ShapeDtypeStruct((1, SLOTS), F32), i...  42.8 us
    unnamed x1, local copies, waits for them, and re-layouts  1.19 us

profile of v3, /device:TPU:1, one launch (start us, length us, event | category | flops | bytes accessed | tf_op | source)
XLA Modules:
  0.0 44.6 jit_solution(2676837399354805894)
XLA Ops:
  0.7 42.8 %shard_map.100 = f32[1,64]{1,0:T(1,128)} custom-call(bf16[64,32,1024]{2,1,0:T(8,128)(2,1)} %passages.1, bf16[1024,1024]{1,0:T(8,128)(2,1)} %query_weight.1, bf16[1024,1024]{1,0:T(8,128)(2,1)} %kv_weight.1, bf16[1024,1024]{1,0:T(8,128)(2,1)} %out_weight.1, bf16[8,128]{1,0:T(8,128)(2,1)} %bitcast.4, bf16[512,1024]{1,0:T(8,128)(2,1)} %bitcast.3, ...), custom_call_target="tpu_custom_call" | custom-call | flops 6000000000 | bytes 12582912 | tf_op jit(solution)/shard_map/pallas_call | solution.py:376
  43.4 1.2 %copy.13 = f32[1,64]{1,0:T(1,128)} copy(f32[1,64]{1,0:T(1,128)} %shard_map.100) | data formatting | bytes 512

commit v4 on v3

--- a/solution.py
+++ b/solution.py
@@ -74,9 +74,9 @@
     passages, query_weight, kv_weight, out_weight, score_vector, prefix, table,
     owner, row, count, out,
     pas, ends, wq, wkv, wo, pre_v, tab, tail,
-    last32, own_rows, own_share, heads_all, pre_keys, req_out, req_in, pick, place,
+    last32, own_rows, own_query, own_share, heads_all, pre_keys, req_out, req_in, pick, place,
     last_out, last_in, sums_out, sums_in, query_all, part_out, part_in, slot_last,
-    owner_row, row_row, score_v, load_sem, send_sem, recv_sem,
+    tot_out, tot_in, owner_row, row_row, score_v, load_sem, send_sem, recv_sem,
 ):
     me = lax.axis_index("corpus")
     px = lax.axis_index("pre")
@@ -185,6 +185,10 @@
         ]
         return jnp.concatenate(parts, axis=0)
 
+    normed = unit(last32[pl.ds(pl.multiple_of(px * BLOCK, BLOCK), BLOCK), :]).astype(BF)
+    for g in range(GROUPS):
+        own_query[g] = query_of(normed, g)
+
     def to_row(ref, channel, at=()):
         for k in (2, 1, 3):
             to = lax.rem(px + k, PRE)
@@ -230,7 +234,6 @@
     sine = jnp.broadcast_to(tail_sin[None], (BLOCK, TOKENS, HEAD)).reshape(CHUNK, HEAD)
     shape = (2 * BLOCK, CHUNK)
     own = (iota(shape, 0) % BLOCK) == (iota(shape, 1) // TOKENS)
-    normed = unit(last32[pl.ds(pl.multiple_of(px * BLOCK, BLOCK), BLOCK), :]).astype(BF)
     for pair in range(GROUPS // 2):
         cols = slice(2 * pair * HEAD, 2 * (pair + 1) * HEAD)
         v_cols = slice((GROUPS + 2 * pair) * HEAD, (GROUPS + 2 * (pair + 1)) * HEAD)
@@ -240,7 +243,7 @@
             g = 2 * pair + i
             keys = turn(unit(both_keys[:, i * HEAD : (i + 1) * HEAD]), cosine, sine).astype(BF)
             values = both_values[:, i * HEAD : (i + 1) * HEAD]
-            expo = jnp.where(own, jnp.exp(dot_t(query_of(normed, g), keys) * SCALE), 0.0)
+            expo = jnp.where(own, jnp.exp(dot_t(own_query[g], keys) * SCALE), 0.0)
             weighted = dot(expo.astype(BF), values).astype(BF)
             high, low = split_two(jnp.sum(expo, axis=1, keepdims=True))
             total = jnp.where(iota((2 * BLOCK, HEAD), 1) < 64, high, low).astype(BF)
@@ -263,9 +266,12 @@
     spread(last_out, last_in, 1)
     prefix_keys(range(WHOLE, GROUPS))
     wait_for(own_share.at[pl.ds(0, PRE - 1)], recv_sem.at[3])
-    for i in range(2):
-        served = dot(pick[...], own_share[:, i].reshape(HEADS * PASS, HEAD)).astype(BF)
-        sums_out[:, i * 16 : (i + 1) * 16, :] = served.reshape(OWNERS, 16, 128)
+    shares = [own_share[:, i].reshape(HEADS * PASS, HEAD) for i in range(2)]
+    served = dot(pick[...], jnp.concatenate(shares, axis=1))
+    sums_out[...] = served[:, 0:128].astype(BF).reshape(OWNERS, 16, 128)
+    total = served[:, 128:129] + served[:, 192:193]
+    total = jnp.where(iota(shape, 1) == (iota(shape, 0) & 15), total, 0.0)
+    tot_out[...] = jnp.sum(total.reshape(OWNERS, 16, 128), axis=1, keepdims=True)
     spread(sums_out, sums_in, 2)
 
     wait_for(last_in.at[pl.ds(0, OWNERS - 1)], recv_sem.at[1])
@@ -278,19 +284,10 @@
         query_all[g, px] = query_of(normed, g)
         if g >= WHOLE:
             to_row(query_all.at[g], 4 + g)
+    spread(tot_out, tot_in, 12)
 
     diagonal = iota((HEAD, HEAD), 0) == iota((HEAD, HEAD), 1)
     whole = []
-    for g in range(WHOLE):
-        wait_for(heads_all.at[g, pl.ds(0, PRE - 1), 0], recv_sem.at[4 + g])
-        wait_for(heads_all.at[g, pl.ds(0, PRE - 1), 1], recv_sem.at[8 + g])
-        weighted = jnp.zeros((2 * SLOTS, HEAD), F32)
-        total = jnp.zeros((2 * SLOTS, 1), F32)
-        for q in range(PRE):
-            expo = jnp.exp(dot_t(query_all[g, px], heads_all[g, q, 0]) * SCALE)
-            weighted = weighted + dot(expo.astype(BF), heads_all[g, q, 1])
-            total = total + jnp.sum(expo, axis=1, keepdims=True)
-        whole.append((weighted, total))
     for g in range(WHOLE, GROUPS):
         wait_for(query_all.at[g, pl.ds(0, PRE - 1)], recv_sem.at[4 + g])
         values = pre_v[:, (GROUPS + g) * HEAD : (GROUPS + g + 1) * HEAD]
@@ -315,14 +312,34 @@
                 device_id_type=MESH,
             ).start()
 
+    for g in range(WHOLE):
+        wait_for(heads_all.at[g, pl.ds(0, PRE - 1), 0], recv_sem.at[4 + g])
+        wait_for(heads_all.at[g, pl.ds(0, PRE - 1), 1], recv_sem.at[8 + g])
+        weighted = jnp.zeros((2 * SLOTS, HEAD), F32)
+        total = jnp.zeros((2 * SLOTS, 1), F32)
+        for q in range(PRE):
+            expo = jnp.exp(dot_t(query_all[g, px], heads_all[g, q, 0]) * SCALE)
+            weighted = weighted + dot(expo.astype(BF), heads_all[g, q, 1])
+            total = total + jnp.sum(expo, axis=1, keepdims=True)
+        whole.append((weighted, total))
     wait_for(sums_in.at[pl.ds(0, OWNERS - 1)], recv_sem.at[2])
-    own_w = dot(place[...], sums_in[:, 0:16, :].reshape(OWNERS * 16, 128))
-    own_t = dot(place[...], sums_in[:, 16:32, :].reshape(OWNERS * 16, 128))
-    own_t = own_t[:, 0:1] + own_t[:, 64:65]
+    wait_for(tot_in.at[pl.ds(0, OWNERS - 1)], recv_sem.at[12])
+    shape = (OWNERS * 16, 128)
+    total = jnp.broadcast_to(tot_in[...], (OWNERS, 16, 128)).reshape(shape)
+    total = jnp.where(iota(shape, 1) == (iota(shape, 0) & 15), total, 0.0)
+    high, low = split_two(jnp.sum(total, axis=1, keepdims=True))
+    total = jnp.where(iota(shape, 1) < 64, high, low).astype(BF)
+    got = dot(place[...], jnp.concatenate([sums_in[...].reshape(shape), total], axis=1))
+    own_w = got[:, 0:128]
+    own_t = got[:, 128:129] + got[:, 192:193]
     copies[9].wait()
     copies[10].wait()
     mixed = []
     for g in range(GROUPS):
+        if g == GROUPS - 1:
+            part = jnp.concatenate(mixed, axis=1)
+            slot_last[...] = slot_last[...] + dot(part, wo[0 : 2 * g * HEAD, :])
+            mixed = []
         rows = slice(g * 2 * SLOTS, (g + 1) * 2 * SLOTS)
         if g < WHOLE:
             weighted, total = whole[g]
@@ -339,7 +356,8 @@
         total = total + own_t[rows]
         result = (weighted / total).astype(BF)
         mixed += [result[0:SLOTS], result[SLOTS:]]
-    updated = slot_last[...] + dot(jnp.concatenate(mixed, axis=1), wo[...])
+    part = dot(jnp.concatenate(mixed, axis=1), wo[WIDTH - 2 * HEAD :, :])
+    updated = slot_last[...] + part
     square = jnp.mean(updated * updated, axis=-1, keepdims=True)
     weights = score_v[...].astype(F32)
     weights = jnp.concatenate([weights[j : j + 1, :] for j in range(8)], axis=1)
@@ -352,6 +370,7 @@
     wait_for(req_out.at[pl.ds(0, OWNERS - 1)], send_sem.at[0])
     wait_for(last_out.at[pl.ds(0, OWNERS - 1)], send_sem.at[1])
     wait_for(sums_out.at[pl.ds(0, OWNERS - 1)], send_sem.at[2])
+    wait_for(tot_out.at[pl.ds(0, OWNERS - 1)], send_sem.at[12])
     wait_for(own_share.at[pl.ds(0, PRE - 1)], send_sem.at[3])
     for g in range(WHOLE):
         wait_for(heads_all.at[g, pl.ds(0, PRE - 1), 0], send_sem.at[4 + g])
@@ -389,6 +408,7 @@
             pltpu.VMEM((TOKENS, HEAD), F32),
             pltpu.VMEM((PASS, WIDTH), F32),
             pltpu.VMEM((8 * PASS, 128), BF),
+            pltpu.VMEM((GROUPS, 2 * BLOCK, HEAD), BF),
             pltpu.VMEM((PRE, 2, HEADS, BLOCK, HEAD), BF),
             pltpu.VMEM((max(WHOLE, 1), PRE, 2, SHARE, HEAD), BF),
             pltpu.VMEM((GROUPS, SHARE, HEAD), BF),
@@ -398,18 +418,20 @@
             pltpu.VMEM((8 * SLOTS, OWNERS * 16), BF),
             pltpu.VMEM((OWNERS, 16, 128), BF),
             pltpu.VMEM((OWNERS, 16, 128), BF),
-            pltpu.VMEM((OWNERS, 32, 128), BF),
-            pltpu.VMEM((OWNERS, 32, 128), BF),
+            pltpu.VMEM((OWNERS, 16, 128), BF),
+            pltpu.VMEM((OWNERS, 16, 128), BF),
             pltpu.VMEM((GROUPS, PRE, 2 * SLOTS, HEAD), BF),
             pltpu.VMEM((GROUPS, PRE, PART, HEAD), BF),
             pltpu.VMEM((GROUPS, PRE, PART, HEAD), BF),
             pltpu.VMEM((SLOTS, WIDTH), F32),
+            pltpu.VMEM((OWNERS, 1, 128), F32),
+            pltpu.VMEM((OWNERS, 1, 128), F32),
             pltpu.VMEM((1, SLOTS), jnp.int32),
             pltpu.VMEM((1, SLOTS), jnp.int32),
             pltpu.VMEM((8, 128), BF),
             pltpu.SemaphoreType.DMA((11,)),
-            pltpu.SemaphoreType.DMA((12,)),
-            pltpu.SemaphoreType.DMA((12,)),
+            pltpu.SemaphoreType.DMA((13,)),
+            pltpu.SemaphoreType.DMA((13,)),
         ],
         compiler_params=pltpu.CompilerParams(
             collective_id=0, has_side_effects=True, vmem_limit_bytes=VLIM * 2**20

time: 44.7 us -> 44.4 us (level)
  no operation moved by 1% of the time
where the time goes in v4:
time: 44.4 us; the launch traced here: 44.3 us
  Pallas kernels  42.5 us (96%)
  local copies, waits for them, and re-layouts  1.19 us (3%)
  between operations  0.66 us (1%)
    pallas_call x1, Pallas kernels, per_device(): pl.pallas_call(kernel, out_shape=jax.ShapeDtypeStruct((1, SLOTS), F32), i...  42.5 us
    unnamed x1, local copies, waits for them, and re-layouts  1.19 us

profile of v4, /device:TPU:1, one launch (start us, length us, event | category | flops | bytes accessed | tf_op | source)
XLA Modules:
  0.0 44.3 jit_solution(8727815194941868788)
XLA Ops:
  0.7 42.5 %shard_map.100 = f32[1,64]{1,0:T(1,128)} custom-call(bf16[64,32,1024]{2,1,0:T(8,128)(2,1)} %passages.1, bf16[1024,1024]{1,0:T(8,128)(2,1)} %query_weight.1, bf16[1024,1024]{1,0:T(8,128)(2,1)} %kv_weight.1, bf16[1024,1024]{1,0:T(8,128)(2,1)} %out_weight.1, bf16[8,128]{1,0:T(8,128)(2,1)} %bitcast.4, bf16[512,1024]{1,0:T(8,128)(2,1)} %bitcast.3, ...), custom_call_target="tpu_custom_call" | custom-call | flops 6000000000 | bytes 12582912 | tf_op jit(solution)/shard_map/pallas_call | solution.py:395
  43.1 1.2 %copy.13 = f32[1,64]{1,0:T(1,128)} copy(f32[1,64]{1,0:T(1,128)} %shard_map.100) | data formatting | bytes 512

commit v5 on v4

--- a/solution.py
+++ b/solution.py
@@ -219,7 +219,7 @@
                 else:
                     pre_keys[g, span, :] = keys
 
-    prefix_keys(range(WHOLE))
+    prefix_keys(range(GROUPS))
 
     pl.semaphore_wait(barrier, OWNERS - 1 + PRE - 1)
     for g in range(WHOLE):
@@ -264,7 +264,6 @@
     pick[...] = jnp.where(iota((OWNERS * 16, 8 * PASS), 1) == asked, 1.0, 0.0).astype(BF)
     last_out[...] = dot(pick[...], own_rows[...]).astype(BF).reshape(OWNERS, 16, 128)
     spread(last_out, last_in, 1)
-    prefix_keys(range(WHOLE, GROUPS))
     wait_for(own_share.at[pl.ds(0, PRE - 1)], recv_sem.at[3])
     shares = [own_share[:, i].reshape(HEADS * PASS, HEAD) for i in range(2)]
     served = dot(pick[...], jnp.concatenate(shares, axis=1))

time: 44.4 us -> 44.3 us (level)
  no operation moved by 1% of the time
where the time goes in v5:
time: 44.3 us; the launch traced here: 44.2 us
  Pallas kernels  42.4 us (96%)
  local copies, waits for them, and re-layouts  1.19 us (3%)
  between operations  0.66 us (1%)
    pallas_call x1, Pallas kernels, per_device(): pl.pallas_call(kernel, out_shape=jax.ShapeDtypeStruct((1, SLOTS), F32), i...  42.4 us
    unnamed x1, local copies, waits for them, and re-layouts  1.19 us

profile of v5, /device:TPU:1, one launch (start us, length us, event | category | flops | bytes accessed | tf_op | source)
XLA Modules:
  0.0 44.2 jit_solution(699560799984647866)
XLA Ops:
  0.7 42.4 %shard_map.100 = f32[1,64]{1,0:T(1,128)} custom-call(bf16[64,32,1024]{2,1,0:T(8,128)(2,1)} %passages.1, bf16[1024,1024]{1,0:T(8,128)(2,1)} %query_weight.1, bf16[1024,1024]{1,0:T(8,128)(2,1)} %kv_weight.1, bf16[1024,1024]{1,0:T(8,128)(2,1)} %out_weight.1, bf16[8,128]{1,0:T(8,128)(2,1)} %bitcast.4, bf16[512,1024]{1,0:T(8,128)(2,1)} %bitcast.3, ...), custom_call_target="tpu_custom_call" | custom-call | flops 6000000000 | bytes 12582912 | tf_op jit(solution)/shard_map/pallas_call | solution.py:394
  43.0 1.2 %copy.13 = f32[1,64]{1,0:T(1,128)} copy(f32[1,64]{1,0:T(1,128)} %shard_map.100) | data formatting | bytes 512
